TPU v7x, 1024 devices: a whole 4x8x16 slice. The times are simulated.
1024 devices in a mesh: section: 4 (over x), seq: 256 (over z, y, core).
Axes of the slice: x: 4, y: 8, z: 16, core: 2. Of those that a mesh axis runs over, the one named last changes fastest.
Arguments:
- queries: bfloat16 [4, 32768, 3072], P('section', 'seq'), may hold values from -60 to 60
- packed_key_value: bfloat16 [4, 32768, 1024], P('section', 'seq'), may hold values from -6 to 6
- incoming: bfloat16 [4, 32768, 3072], P('section', 'seq'), may hold values from -6 to 6
- loss_grad: bfloat16 [32768, 3072], P('seq'), may hold values from -6 to 6
- global_blocks: int32 [4, 2], P('section'), may hold values from 0 to 511
- random_blocks: int32 [4, 512, 4, 3], P('section'), may hold values from 0 to 511, as said below
Outputs:
- d_queries: bfloat16 [4, 32768, 3072], P('section', 'seq')
- d_key_value: bfloat16 [4, 32768, 1024], P('section', 'seq')
Inputs may be any that keep to these rules, and one draw needn't show every extreme that they name: `random_blocks`: the random blocks of a query block lie among the blocks held by the seq index that holds the query block and the indices just before and after it.
All inputs are finite; a program needn't handle non-finite values.
Results may differ from a plain program's by a relative error of at most 0.006.
Values may be sent and summed in bfloat16 or wider, within the bound.
A program may use at most 32 MiB of HBM per device.

v0:
```python
import math

import jax
import jax.numpy as jnp
from jax import lax
from jax.sharding import PartitionSpec as P

HQ = 24
KEY_HEADS = 4
HEAD_SIZE = 128
BLOCK_TOKENS = 64
GLOBAL_BLOCKS = 2
RANDOM_BLOCKS = 3
GROUP_HEADS = 6


def from_behind(shard, axis, by):
    peers = lax.axis_size(axis)
    pairs = [(i, i + by) for i in range(peers) if 0 <= i + by < peers]
    return lax.ppermute(shard, axis, pairs)


def with_halo(shard, sides, width):
    for axis, dim in sides:
        peers, length = (lax.axis_size(axis), shard.shape[dim])
        up = [(i, (i + 1) % peers) for i in range(peers - 1)]
        down = [(j, i) for i, j in up]
        last = lax.slice_in_dim(shard, length - width, length, axis=dim)
        first = lax.slice_in_dim(shard, 0, width, axis=dim)
        before = lax.ppermute(last, axis, up)
        after = lax.ppermute(first, axis, down)
        shard = jnp.concatenate([before, shard, after], axis=dim)
    return shard


def body(queries, packed_key_value, incoming, loss_grad, global_blocks, random_blocks):
    score_scale = 1.0 / math.sqrt(HEAD_SIZE)
    tok_rows = queries.shape[1]
    local_block_count = tok_rows // BLOCK_TOKENS
    width_kv = packed_key_value.shape[2]
    position = lax.axis_index("seq")
    seq_count = lax.axis_size("seq")
    every_block = local_block_count * seq_count
    shifted = from_behind(incoming, "section", -1)
    is_last = lax.axis_index("section") == lax.axis_size("section") - 1
    output_gradient = jnp.where(is_last, loss_grad, shifted[0])
    pairs_own = packed_key_value[0]
    extended = with_halo(pairs_own, (("seq", 0),), tok_rows)
    global_block_index = global_blocks[0]
    random_table = random_blocks[0]
    owners_of = global_block_index // local_block_count
    local_slot = global_block_index % local_block_count
    own_blocks = pairs_own.reshape(local_block_count, BLOCK_TOKENS, width_kv)
    pick_mask = (
        (owners_of[:, None] == position)
        & (local_slot[:, None] == jnp.arange(local_block_count, dtype=jnp.int32)[None, :])
    ).astype(jnp.float32)
    owned_rows = jnp.einsum(
        "gn,nkc->gkc", pick_mask, own_blocks.astype(jnp.float32), precision=lax.Precision.HIGHEST
    )
    glob_rows = lax.psum(owned_rows, "seq").astype(jnp.bfloat16)
    candidate_blocks = jnp.concatenate(
        [extended.reshape(3 * local_block_count, BLOCK_TOKENS, width_kv), glob_rows], 0
    )
    candidate_count = 3 * local_block_count + GLOBAL_BLOCKS
    candidate_groups = candidate_blocks.reshape(
        candidate_count, BLOCK_TOKENS, 2, KEY_HEADS, HEAD_SIZE
    ).transpose(3, 0, 1, 2, 4)
    block_ids = jnp.arange(local_block_count, dtype=jnp.int32)
    offsets = jnp.arange(-1, 2, dtype=jnp.int32)[None, :]
    global_ids = position * local_block_count + block_ids[:, None] + offsets
    usable = jnp.concatenate(
        [
            (global_ids >= 0) & (global_ids < every_block),
            jnp.ones((local_block_count, GLOBAL_BLOCKS + RANDOM_BLOCKS), dtype=bool),
        ],
        1,
    )
    key_mask = jnp.repeat(usable, BLOCK_TOKENS, axis=1)
    window_blocks = local_block_count + block_ids[:, None] + offsets
    global_slot_rows = 3 * local_block_count + jnp.arange(GLOBAL_BLOCKS, dtype=jnp.int32)
    own_random = lax.dynamic_slice_in_dim(
        random_table, position * local_block_count, local_block_count, 0
    )
    random_block_index = jnp.transpose(own_random, (1, 0, 2)) - (position - 1) * local_block_count
    key_block_index = jnp.concatenate(
        [
            jnp.broadcast_to(window_blocks[None], (KEY_HEADS, local_block_count, 3)),
            jnp.broadcast_to(
                global_slot_rows[None, None, :], (KEY_HEADS, local_block_count, GLOBAL_BLOCKS)
            ),
            random_block_index,
        ],
        2,
    )
    query_group_rows = (
        queries[0]
        .reshape(local_block_count, BLOCK_TOKENS, KEY_HEADS, GROUP_HEADS, HEAD_SIZE)
        .transpose(2, 0, 1, 3, 4)
    )
    gradient_group_rows = output_gradient.reshape(
        local_block_count, BLOCK_TOKENS, KEY_HEADS, GROUP_HEADS, HEAD_SIZE
    ).transpose(2, 0, 1, 3, 4)
    cand_range = jnp.arange(candidate_count, dtype=jnp.int32)

    def one_group(group_args):
        index_g, query_grouped, gradient_grouped, pairs_g = group_args
        selected = pairs_g[index_g]
        key_row_block = selected[:, :, :, 0].reshape(local_block_count, -1, HEAD_SIZE)
        value_row_block = selected[:, :, :, 1].reshape(local_block_count, -1, HEAD_SIZE)
        logit_scores = (
            jnp.einsum(
                "elmi,eti->emlt", query_grouped, key_row_block, preferred_element_type=jnp.float32
            )
            * score_scale
        )
        logit_scores = jnp.where(key_mask[:, None, None, :], logit_scores, -1e30)
        row_max = jnp.max(logit_scores, axis=-1, keepdims=True)
        weights_raw = jnp.exp(logit_scores - row_max)
        row_total = jnp.sum(weights_raw, axis=-1, keepdims=True)
        probs = weights_raw / row_total
        probability_lowbits = probs.astype(jnp.bfloat16)
        probability_gradient = jnp.einsum(
            "elmi,eti->emlt", gradient_grouped, value_row_block, preferred_element_type=jnp.float32
        )
        row_delta = jnp.sum(probs * probability_gradient, axis=-1, keepdims=True)
        score_gradient = (probs * (probability_gradient - row_delta) * score_scale).astype(
            jnp.bfloat16
        )
        query_gradient = jnp.einsum(
            "yzmu,yup->ymzp", score_gradient, key_row_block, preferred_element_type=jnp.float32
        )
        key_gradient = jnp.einsum(
            "xapt,xpag->xtg", score_gradient, query_grouped, preferred_element_type=jnp.float32
        )
        value_gradient = jnp.einsum(
            "xapt,xpag->xtg",
            probability_lowbits,
            gradient_grouped,
            preferred_element_type=jnp.float32,
        )
        paired = jnp.stack([key_gradient, value_gradient], 2).reshape(
            -1, BLOCK_TOKENS * 2 * HEAD_SIZE
        )
        onehot = (index_g.reshape(-1)[:, None] == cand_range[None, :]).astype(jnp.float32)
        summed = jnp.dot(onehot.T, paired, precision=lax.Precision.HIGHEST)
        stats_g = jnp.stack([row_max[..., 0], row_total[..., 0], row_delta[..., 0]], 0)
        return (query_gradient, summed, stats_g)

    grad_query_all, reduced_total, stats_all = lax.map(
        one_group, (key_block_index, query_group_rows, gradient_group_rows, candidate_groups)
    )
    d_queries = (
        grad_query_all.transpose(1, 2, 0, 3, 4)
        .reshape(tok_rows, HQ * HEAD_SIZE)
        .astype(jnp.bfloat16)
    )
    cand_grads = (
        reduced_total.reshape(KEY_HEADS, candidate_count, BLOCK_TOKENS, 2, HEAD_SIZE)
        .transpose(1, 2, 3, 0, 4)
        .reshape(candidate_count, BLOCK_TOKENS, width_kv)
    )
    glob_grads = cand_grads[3 * local_block_count :]
    shard_grads = cand_grads[: 3 * local_block_count].reshape(3 * tok_rows, width_kv)
    returned = with_halo(shard_grads, (("seq", 0),), tok_rows)
    own_grad = (
        returned[2 * tok_rows : 3 * tok_rows] + returned[:tok_rows] + returned[4 * tok_rows :]
    )
    global_sum = lax.psum(glob_grads, "seq")
    own_grad = own_grad + jnp.einsum(
        "gn,gkc->nkc", pick_mask, global_sum, precision=lax.Precision.HIGHEST
    ).reshape(tok_rows, width_kv)
    return (d_queries[None], own_grad.astype(jnp.bfloat16)[None])


def solution(mesh):
    in_specs = (
        P("section", "seq", None),
        P("section", "seq", None),
        P("section", "seq", None),
        P("seq", None),
        P("section", None),
        P("section", None, None, None),
    )
    out_specs = (P("section", "seq", None), P("section", "seq", None))
    return jax.shard_map(body, mesh=mesh, in_specs=in_specs, out_specs=out_specs, check_vma=False)
```

profile of v0, /device:TPU:1, one launch (start us, length us, event | category | flops | bytes accessed | tf_op | source)
XLA Modules:
  0.0 1475.8 jit_solution(5649830001997710158)
XLA Ops:
  7.2 16.2 %collective-permute-start.1 = (bf16[128,1024]{1,0:T(8,128)(2,1)}, bf16[128,1024]{1,0:T(8,128)(2,1)S(1)}, u32[]{:S(2)}, u32[]{:S(2)}) collective-permute-start(bf16[128,1024]{1,0:T(8,128)(2,1)} %bitcast.210), channel_id=1, source_target_pairs={{1,0},{2,1},{3,2},{4,3},{5,4},{6,5},{7,6},{8,7},{9,8},{10,9},{11,1... | collective-permute-start | bytes 786440 | tf_op jit(solution)/shard_map/ppermute | solution.py:31
  23.4 1.9 collective-permute-start
  25.4 1.3 collective-permute-start.2
  26.7 0.7 and_select_fusion
  27.4 0.7 fusion.59
  28.0 1.5 fusion.57
  29.5 980.7 %all-reduce.5 = bf16[2,64,1024]{2,0,1:T(2,128)(2,1)S(1)} all-reduce(f32[2,64,1024]{2,0,1:T(2,128)S(1)} %fusion.57), channel_id=1, replica_groups=mesh['section'=4,'seq'=256] {'seq'}, use_global_device_ids=true, to_apply=%region_0.1 | all-reduce | flops 131072 | bytes 786432 | tf_op jit(solution)/shard_map/psum | solution.py:61
  1011.2 0.9 reshape_squeeze.7
  1012.2 1.2 copy.48
  1013.5 1.0 pad_maximum_fusion.1
  1014.5 0.6 concatenate.18
  1015.1 0.5 maximum_bitcast_fusion
  1015.5 1.2 copy.46
  1016.9 0.9 reshape.176
  1018.1 96.2 %while.13 = (s32[]{:T(128)}, bf16[4,2,64,6,128]{4,2,3,1,0:T(8,128)(2,1)}, f32[4,8,16384]{2,1,0:T(8,128)}, bf16[4,8,64,2,128]{4,2,3,1,0:T(8,128)(2,1)}, s32[4,2,8...) while((s32[]{:T(128)}, ...), condition=%wide.region_5.6_spmd.clone, body=%wide.region_1.5_spmd.clone.sunk | while | flops 638457280 | bytes 29743888 | solution.py:150
  1018.3 1.0 dynamic-slice_bitcast_fusion.2
  1019.4 0.6 gather_fusion
  1020.1 0.4 fusion.103
  1020.6 2.7 fusion.104
  1023.3 6.3 fusion.105
  1029.6 2.7 convolution_bitcast_fusion.6
  1032.4 6.8 convolution_bitcast_fusion.7
  1039.2 0.8 copy.72
  1040.0 0.8 reshape.207
  1041.0 1.3 fusion.106
  1042.3 1.0 dynamic-slice_bitcast_fusion.2
  1043.4 0.6 gather_fusion
  1044.1 0.4 fusion.103
  1044.6 2.6 fusion.104
  1047.3 6.4 fusion.105
  1053.6 2.7 convolution_bitcast_fusion.6
  1056.4 6.8 convolution_bitcast_fusion.7
  1063.2 0.8 copy.72
  1064.0 0.8 reshape.207
  1065.0 1.4 fusion.106
  1066.3 1.0 dynamic-slice_bitcast_fusion.2
  1067.4 0.6 gather_fusion
  1068.1 0.4 fusion.103
  1068.6 2.7 fusion.104
  1071.3 6.3 fusion.105
  1077.7 2.7 convolution_bitcast_fusion.6
  1080.4 6.8 convolution_bitcast_fusion.7
  1087.2 0.8 copy.72
  1088.1 0.8 reshape.207
  1089.0 1.4 fusion.106
  1090.4 1.0 dynamic-slice_bitcast_fusion.2
  1091.4 0.6 gather_fusion
  1092.1 0.4 fusion.103
  1092.7 2.6 fusion.104
  1095.3 6.3 fusion.105
  1101.7 2.7 convolution_bitcast_fusion.6
  1104.4 6.8 convolution_bitcast_fusion.7
  1111.2 0.8 copy.72
  1112.1 0.8 reshape.207
  1113.0 1.4 fusion.106
  1114.4 2.9 copy.70
  1117.9 7.6 collective-permute-start.4
  1125.8 2.1 collective-permute-start.3
  1127.9 1.2 slice.42
  1129.2 0.5 copy.50
  1129.7 1.7 convert_element_type.34
  1131.7 332.9 %all-reduce.4.cloned.1.call-done = f32[2,64,1024]{2,0,1:T(2,128)} async-done(((f32[2,64,1024]{2,0,1:T(2,128)}), f32[2,64,1024]{2,0,1:T(2,128)}) %all-reduce.4.cloned.1.call-update) | async-done | bytes 524304 | tf_op jit(solution)/shard_map/psum | solution.py:169
  1464.6 2.1 fusion.60
  1466.9 2.1 fusion.56
  (78 shorter events, 4.6 us)
Async XLA Ops:
  7.2 1003.1 %copy-start = (s32[1,512,4,3]{1,2,3,0:T(4,128)S(1)}, s32[1,512,4,3]{1,2,3,0:T(4,128)}, u32[]{:S(2)}) copy-start(s32[1,512,4,3]{1,2,3,0:T(4,128)} %param.13) | copy-start | bytes 73732
  7.2 1004.0 %copy-start.1 = (bf16[1,128,3072]{2,1,0:T(8,128)(2,1)S(1)}, bf16[1,128,3072]{2,1,0:T(8,128)(2,1)}, u32[]{:S(2)}) copy-start(bf16[1,128,3072]{2,1,0:T(8,128)(2,1)} %param.8) | copy-start | bytes 2359300
  7.2 1457.4 %all-reduce.4.cloned.1.call-start = ((), (), s32[]{:S(2)}) async-start(), calls=%async_computation | async-start | bytes 1048576 | tf_op jit(solution)/shard_map/psum | solution.py:169
  7.2 1006.2 %collective-permute-start.1 = (bf16[128,1024]{1,0:T(8,128)(2,1)}, bf16[128,1024]{1,0:T(8,128)(2,1)S(1)}, u32[]{:S(2)}, u32[]{:S(2)}) collective-permute-start(bf16[128,1024]{1,0:T(8,128)(2,1)} %bitcast.210), channel_id=1, source_target_pairs={{1,0},{2,1},{3,2},{4,3},{5,4},{6,5},{7,6},{8,7},{9,8},{10,9},{11,1... | collective-permute-start | bytes 786440 | tf_op jit(solution)/shard_map/ppermute | solution.py:31
  23.4 990.0 %collective-permute-start = (bf16[128,1024]{1,0:T(8,128)(2,1)}, bf16[128,1024]{1,0:T(8,128)(2,1)}, u32[]{:S(2)}, u32[]{:S(2)}) collective-permute-start(bf16[128,1024]{1,0:T(8,128)(2,1)} %bitcast.211), channel_id=1, source_target_pairs={{0,1},{1,2},{2,3},{3,4},{4,5},{5,6},{6,7},{7,8},{8,9},{9,10},{10,1... | collective-permute-start | bytes 786440 | tf_op jit(solution)/shard_map/ppermute | solution.py:30
  25.4 991.4 %collective-permute-start.2 = (bf16[1,128,3072]{2,1,0:T(8,128)(2,1)}, bf16[1,128,3072]{2,1,0:T(8,128)(2,1)S(1)}, u32[]{:S(2)}, u32[]{:S(2)}) collective-permute-start(bf16[1,128,3072]{2,1,0:T(8,128)(2,1)} %param.10), channel_id=1, source_target_pairs={{256,0},{512,256},{768,512},{257,1},{513,257},{769,513},{258,2},{5... | collective-permute-start | bytes 2359304 | tf_op jit(solution)/shard_map/ppermute | solution.py:20
  1011.2 2.3 copy-start.4
  1015.0 1.7 copy-start.2
  1117.9 348.9 %collective-permute-start.4 = (f32[128,1024]{1,0:T(8,128)S(1)}, f32[128,1024]{1,0:T(8,128)}, u32[]{:S(2)}, u32[]{:S(2)}) collective-permute-start(f32[128,1024]{1,0:T(8,128)S(1)} %slice.40), channel_id=1, source_target_pairs={{1,0},{2,1},{3,2},{4,3},{5,4},{6,5},{7,6},{8,7},{9,8},{10,9},{11,1... | collective-permute-start | bytes 1572872 | tf_op jit(solution)/shard_map/ppermute | solution.py:31
  1125.6 3.6 copy-start.3
  1125.8 341.1 %collective-permute-start.3 = (f32[128,1024]{1,0:T(8,128)S(1)}, f32[128,1024]{1,0:T(8,128)}, u32[]{:S(2)}, u32[]{:S(2)}) collective-permute-start(f32[128,1024]{1,0:T(8,128)S(1)} %slice.38), channel_id=1, source_target_pairs={{0,1},{1,2},{2,3},{3,4},{4,5},{5,6},{6,7},{7,8},{8,9},{9,10},{10,1... | collective-permute-start | bytes 1572872 | tf_op jit(solution)/shard_map/ppermute | solution.py:30
Sparse Core Ops, SparseCore 0:
  1129.3 335.2 all-reduce.3
where the time goes:
time: 1480 us
  blocking collectives  981 us (66%)
  waiting for transfers between devices  333 us (22%)
  matrix products  84.4 us (6%)
  starting transfers between devices  29.2 us (2%)
  local copies, waits for them, and re-layouts  28.2 us (2%)
    psum x1, blocking collectives, body(): glob_rows = lax.psum(owned_rows, 'seq').astype(jnp.bfloat16)  981 us
    psum x1, waiting for transfers between devices, body(): global_sum = lax.psum(glob_grads, 'seq')  333 us
  transfers between devices with their start and end apart: 6, of which 1 were waited for; matrix products, arithmetic and copies ran while one was open for 1% of the time, Pallas kernels for 0%

commit v1 on v0

v1 whole, which is shorter than its diff:
```python
import functools
import math

import jax
import jax.numpy as jnp
from jax import lax
from jax.experimental import pallas as pl
from jax.experimental.pallas import tpu as pltpu
from jax.sharding import PartitionSpec as P

HQ = 24
KEY_HEADS = 4
HEAD = 128
BLOCK = 64
GROUP = 6
TOK = 128
GROUP_COLS = GROUP * HEAD
KEYS = 3 * TOK + 2 * BLOCK
HALVES = 2
PER_HALF = KEY_HEADS // HALVES
MESH = pl.DeviceIdType.MESH
F32 = jnp.float32
BF16 = jnp.bfloat16
SCALE = 1.0 / math.sqrt(HEAD)
LOG2E = math.log2(math.e)


def kernel(
    n_sec, plane, nz,
    q_hbm, kv_hbm, inc_hbm, loss_hbm, gb_ref, rb_ref,
    dq_hbm, dkv_hbm,
    qv, dout, kvo, kvh, bias, kall, vall, kallt,
    g1src, r1a, r1b, r2a, r2b, gkv,
    acc, own, hgs, hgr, g2src, g2r1, g2r2, g2f, dqv, dkvv,
    in_sem, loss_sem, out_sem,
    sh_s, sh_r, ha_s, ha_r, hg_s, hg_r, pl_s, pl_r,
):
    n_seq = plane * nz
    r1, r2 = (r1a, r1b), (r2a, r2b)
    ch = 4 * BLOCK // plane
    rows = min(ch, BLOCK)
    s = lax.axis_index("section")
    q = lax.axis_index("seq")
    z = q // plane
    yc = q % plane
    right = (s, lax.rem(q + 1, n_seq))
    left = (s, lax.rem(q + n_seq - 1, n_seq))
    back = (lax.rem(s + n_sec - 1, n_sec), q)
    ahead = (lax.rem(s + 1, n_sec), q)

    def plane_peer(i):
        k = lax.rem(yc + i, plane)
        return k, (s, z * plane + k)

    def z_peer(i):
        k = lax.rem(z + i, nz)
        return k, (s, k * plane + yc)

    barrier = pltpu.get_barrier_semaphore()
    for peer in (right, left, back, ahead):
        pl.semaphore_signal(barrier, inc=1, device_id=peer, device_id_type=MESH)

    @pl.loop(1, plane)
    def _(i):
        pl.semaphore_signal(barrier, inc=1, device_id=plane_peer(i)[1], device_id_type=MESH)

    @pl.loop(1, nz)
    def _(i):
        pl.semaphore_signal(barrier, inc=1, device_id=z_peer(i)[1], device_id_type=MESH)

    load_kv = pltpu.make_async_copy(kv_hbm.at[0], kvo, in_sem.at[0])
    load_q = pltpu.make_async_copy(q_hbm.at[0], qv, in_sem.at[1])
    load_kv.start()
    load_q.start()

    def cols(g):
        return pl.ds(pl.multiple_of(g * GROUP_COLS, GROUP_COLS), GROUP_COLS)

    def loss_copy(g):
        return pltpu.make_async_copy(loss_hbm.at[:, cols(g)], dout.at[g], loss_sem.at[g])

    @pl.when(s == n_sec - 1)
    def _():
        for g in range(KEY_HEADS):
            loss_copy(g).start()

    pl.semaphore_wait(barrier, 4 + plane - 1 + nz - 1)

    def shift(g):
        return pltpu.make_async_remote_copy(
            inc_hbm.at[0, :, cols(g)], dout.at[g], sh_s.at[g], sh_r.at[g], back, MESH
        )

    @pl.when(s > 0)
    def _():
        for g in range(KEY_HEADS):
            shift(g).start()

    load_kv.wait()
    for j in range(2):
        high = lax.rem(gb_ref[0, j], 2) == 1
        block = jnp.where(high, kvo[BLOCK:, :], kvo[:BLOCK, :])
        for part in range(2):
            for g in range(KEY_HEADS):
                col = part * KEY_HEADS * HEAD + g * HEAD
                for i in range(BLOCK // rows):
                    at = part * 2 * BLOCK + j * BLOCK + i * rows
                    g1src[g // PER_HALF, at // ch, g % PER_HALF, at % ch : at % ch + rows, :] = block[
                        i * rows : (i + 1) * rows, col : col + HEAD
                    ]

    def all_of(buf, count, sem):
        return pltpu.make_async_copy(buf.at[pl.ds(0, count)], buf.at[pl.ds(0, count)], sem)

    def plane_scatter(src, dst, row):
        @pl.loop(1, plane)
        def _(i):
            k, peer = plane_peer(i)
            pltpu.make_async_remote_copy(
                src.at[k], dst.at[yc], pl_s.at[row], pl_r.at[row], peer, MESH
            ).start()

    def plane_gather(buf, row):
        @pl.loop(1, plane)
        def _(i):
            _, peer = plane_peer(i)
            pltpu.make_async_remote_copy(
                buf.at[yc], buf.at[yc], pl_s.at[row], pl_r.at[row], peer, MESH
            ).start()

    def z_gather(buf, row):
        @pl.loop(1, nz)
        def _(i):
            _, peer = z_peer(i)
            pltpu.make_async_remote_copy(
                buf.at[z], buf.at[z], pl_s.at[row], pl_r.at[row], peer, MESH
            ).start()

    for h in range(HALVES):
        plane_scatter(g1src.at[h], r1[h], h)

    halo_right = pltpu.make_async_remote_copy(kv_hbm.at[0], kvh.at[0], ha_s.at[0], ha_r.at[0], right, MESH)
    halo_left = pltpu.make_async_remote_copy(kv_hbm.at[0], kvh.at[1], ha_s.at[1], ha_r.at[1], left, MESH)
    halo_right.start()
    halo_left.start()

    table = rb_ref[...].astype(F32)
    lane = lax.broadcasted_iota(jnp.int32, table.shape, 2)
    first_block = (2 * (q - 1)).astype(F32)
    picks = [
        jnp.sum(jnp.where(lane == 2 * q + b, table, 0.0), axis=2, keepdims=True) - first_block
        for b in range(2)
    ]
    token = lax.broadcasted_iota(jnp.int32, (KEY_HEADS, TOK), 1)
    second = token >= BLOCK
    listed = [jnp.where(second, picks[1][r], picks[0][r]) for r in range(3)]
    middle = jnp.where(second, 3, 2)
    for kb in range(6):
        block_id = 2 * (q - 1) + kb
        usable = (jnp.abs(middle - kb) <= 1) & (block_id >= 0) & (block_id < 2 * n_seq)
        count = jnp.where(usable, 1.0, 0.0)
        for r in range(3):
            count += jnp.where(listed[r] == float(kb), 1.0, 0.0)
        value = jnp.where(count > 3.5, 2.0, jnp.where(count > 2.5, math.log2(3.0), jnp.where(count > 1.5, 1.0, 0.0)))
        value = jnp.where(count > 0.5, value, -1e30)
        for g in range(KEY_HEADS):
            bias[g, kb : kb + 1, :] = value[g : g + 1, :]
    for g in range(KEY_HEADS):
        bias[g, 6:8, :] = jnp.zeros((2, TOK), F32)

    def owner(k, sub):
        j = lax.rem((k * ch + sub * rows) // BLOCK, 2)
        return jnp.where(j == 0, gb_ref[0, 0], gb_ref[0, 1]) // 2

    for h in range(HALVES):
        all_of(r1[h], plane - 1, pl_r.at[h]).wait()
        r1[h][yc] = g1src[h, yc]
        for sub in range(ch // rows):
            holder = lax.rem(owner(yc, sub), plane)
            part = r1[h][holder]
            r2[h][z, :, sub * rows : (sub + 1) * rows, :] = part[:, sub * rows : (sub + 1) * rows, :]
        z_gather(r2[h], 2 + h)
    for h in range(HALVES):
        all_of(r2[h], nz - 1, pl_r.at[2 + h]).wait()
        for sub in range(ch // rows):
            holder = owner(yc, sub) // plane
            part = r2[h][holder]
            gkv[h, yc, :, sub * rows : (sub + 1) * rows, :] = part[:, sub * rows : (sub + 1) * rows, :]
        plane_gather(gkv.at[h], 4 + h)

    load_q.wait()
    halo_right.wait()
    halo_left.wait()

    def store_dq(g):
        return pltpu.make_async_copy(dqv.at[:, cols(g)], dq_hbm.at[0, :, cols(g)], out_sem.at[g])

    def halo_grad(side, g):
        return pltpu.make_async_remote_copy(
            hgs.at[side, g], hgr.at[1 - side, g], hg_s.at[side, g], hg_r.at[1 - side, g],
            left if side == 0 else right, MESH,
        )

    def one_group(h, gg):
        g = h * PER_HALF + gg

        @pl.when(s < n_sec - 1)
        def _():
            shift(g).wait_recv()

        @pl.when(s == n_sec - 1)
        def _():
            loss_copy(g).wait()

        for part, dst in ((0, kall), (1, vall)):
            col = pl.ds(pl.multiple_of((part * KEY_HEADS + g) * HEAD, HEAD), HEAD)
            dst[0:TOK, :] = kvh[0, :, col]
            dst[TOK : 2 * TOK, :] = kvo[:, col]
            dst[2 * TOK : 3 * TOK, :] = kvh[1, :, col]
            half = plane // 2
            dst[3 * TOK :, :] = gkv[h, part * half : (part + 1) * half, gg].reshape(2 * BLOCK, HEAD)
        kallt[...] = kall[...].T
        acc[...] = jnp.zeros_like(acc)
        bias_row = bias[g]
        bias_two = jnp.concatenate([bias_row, bias_row], axis=1)

        @pl.loop(0, GROUP // 2)
        def _(pair):
            at = pl.multiple_of(g * GROUP_COLS + pair * 2 * HEAD, 2 * HEAD)
            here = pl.multiple_of(pair * 2 * HEAD, 2 * HEAD)
            q_wide = qv[:, pl.ds(at, 2 * HEAD)]
            d_wide = dout[g, :, pl.ds(here, 2 * HEAD)]
            q_rows = jnp.concatenate([q_wide[:, :HEAD], q_wide[:, HEAD:]], axis=0)
            d_rows = jnp.concatenate([d_wide[:, :HEAD], d_wide[:, HEAD:]], axis=0)
            scores = lax.dot_general(
                kall[...], q_rows, (((1,), (1,)), ((), ())), preferred_element_type=F32
            )
            scores = (scores * (SCALE * LOG2E)).reshape(8, BLOCK, 2 * TOK) + bias_two[:, None, :]
            scores = scores.reshape(KEYS, 2 * TOK)
            top = jnp.max(scores, axis=0, keepdims=True)
            weights = jnp.exp2(scores - top)
            total = jnp.sum(weights, axis=0, keepdims=True)
            probs = weights * (1.0 / total)
            grad_probs = lax.dot_general(
                vall[...], d_rows, (((1,), (1,)), ((), ())), preferred_element_type=F32
            )
            delta = jnp.sum(probs * grad_probs, axis=0, keepdims=True)
            grad_scores = (probs * (grad_probs - delta) * SCALE).astype(BF16)
            acc[1] += jnp.dot(probs.astype(BF16), d_rows, preferred_element_type=F32)
            acc[0] += jnp.dot(grad_scores, q_rows, preferred_element_type=F32)
            dq_t = jnp.dot(kallt[...], grad_scores, preferred_element_type=F32)
            dq_two = dq_t.T.astype(BF16)
            dqv[:, pl.ds(at, HEAD)] = dq_two[:TOK]
            dqv[:, pl.ds(pl.multiple_of(at + HEAD, HEAD), HEAD)] = dq_two[TOK:]

        store_dq(g).start()
        hgs[0, g] = acc[:, 0:TOK, :]
        own[g] = acc[:, TOK : 2 * TOK, :]
        hgs[1, g] = acc[:, 2 * TOK : 3 * TOK, :]
        half = plane // 2
        for part in range(2):
            g2src[h, part * half : (part + 1) * half, gg] = acc[part, 3 * TOK :, :].reshape(half, ch, HEAD)
        halo_grad(0, g).start()
        halo_grad(1, g).start()

    for h in range(HALVES):
        all_of(gkv.at[h], plane - 1, pl_r.at[4 + h]).wait()

        @pl.loop(0, PER_HALF)
        def _(gg, h=h):
            one_group(h, gg)

        plane_scatter(g2src.at[h], g2r1.at[h], 6 + h)

    for h in range(HALVES):
        all_of(g2r1.at[h], plane - 1, pl_r.at[6 + h]).wait()
        g2r1[h, yc] = g2src[h, yc]
        total = g2r1[h, 0]
        for k in range(1, plane):
            total += g2r1[h, k]
        g2r2[h, z] = total.astype(BF16)
        z_gather(g2r2.at[h], 8 + h)
    for h in range(HALVES):
        all_of(g2r2.at[h], nz - 1, pl_r.at[8 + h]).wait()
        total = g2r2[h, 0].astype(F32)
        for k in range(1, nz):
            total += g2r2[h, k].astype(F32)
        g2f[h, yc] = total.astype(BF16)
        plane_gather(g2f.at[h], 10 + h)

    for g in range(KEY_HEADS):
        for side in range(2):
            halo_grad(side, g).wait_send()
            halo_grad(side, g).wait_recv()
        own[g] += hgr[0, g] + hgr[1, g]
    for h in range(HALVES):
        all_of(g2f.at[h], plane - 1, pl_r.at[10 + h]).wait()
        half = plane // 2
        for gg in range(PER_HALF):
            g = h * PER_HALF + gg
            for part in range(2):
                sums = g2f[h, part * half : (part + 1) * half, gg].reshape(2 * BLOCK, HEAD).astype(F32)
                for n in range(2):
                    grad = own[g, part, n * BLOCK : (n + 1) * BLOCK, :]
                    for j in range(2):
                        mine = gb_ref[0, j] == 2 * q + n
                        grad += jnp.where(mine, sums[j * BLOCK : (j + 1) * BLOCK], 0.0)
                    col = (part * KEY_HEADS + g) * HEAD
                    dkvv[n * BLOCK : (n + 1) * BLOCK, col : col + HEAD] = grad.astype(BF16)
    store_kv = pltpu.make_async_copy(dkvv, dkv_hbm.at[0], out_sem.at[KEY_HEADS])
    store_kv.start()

    @pl.when(s > 0)
    def _():
        for g in range(KEY_HEADS):
            shift(g).wait_send()

    for h in range(HALVES):
        all_of(g1src.at[h], plane - 1, pl_s.at[h]).wait()
        all_of(r2[h], nz - 1, pl_s.at[2 + h]).wait()
        all_of(gkv.at[h], plane - 1, pl_s.at[4 + h]).wait()
        all_of(g2src.at[h], plane - 1, pl_s.at[6 + h]).wait()
        all_of(g2r2.at[h], nz - 1, pl_s.at[8 + h]).wait()
        all_of(g2f.at[h], plane - 1, pl_s.at[10 + h]).wait()
    for g in range(KEY_HEADS):
        store_dq(g).wait()
    store_kv.wait()


def body(n_sec, plane, nz, queries, packed_key_value, incoming, loss_grad, global_blocks, random_blocks):
    ch = 4 * BLOCK // plane
    table = jnp.transpose(random_blocks[0], (2, 1, 0))
    anywhere = pl.BlockSpec(memory_space=pl.ANY)
    vmem = pltpu.VMEM
    dma = pltpu.SemaphoreType.DMA
    wide = 2 * KEY_HEADS * HEAD
    return pl.pallas_call(
        functools.partial(kernel, n_sec, plane, nz),
        out_shape=(
            jax.ShapeDtypeStruct(queries.shape, BF16),
            jax.ShapeDtypeStruct(packed_key_value.shape, BF16),
        ),
        in_specs=[anywhere] * 4 + [pl.BlockSpec(memory_space=pltpu.SMEM), pl.BlockSpec(memory_space=pltpu.VMEM)],
        out_specs=(anywhere, anywhere),
        scratch_shapes=[
            vmem((TOK, HQ * HEAD), BF16),
            vmem((KEY_HEADS, TOK, GROUP_COLS), BF16),
            vmem((TOK, wide), BF16),
            vmem((2, TOK, wide), BF16),
            vmem((KEY_HEADS, 8, TOK), F32),
            vmem((KEYS, HEAD), BF16),
            vmem((KEYS, HEAD), BF16),
            vmem((HEAD, KEYS), BF16),
            vmem((HALVES, plane, PER_HALF, ch, HEAD), BF16),
            vmem((plane, PER_HALF, ch, HEAD), BF16),
            vmem((plane, PER_HALF, ch, HEAD), BF16),
            vmem((nz, PER_HALF, ch, HEAD), BF16),
            vmem((nz, PER_HALF, ch, HEAD), BF16),
            vmem((HALVES, plane, PER_HALF, ch, HEAD), BF16),
            vmem((2, KEYS, HEAD), F32),
            vmem((KEY_HEADS, 2, TOK, HEAD), F32),
            vmem((2, KEY_HEADS, 2, TOK, HEAD), F32),
            vmem((2, KEY_HEADS, 2, TOK, HEAD), F32),
            vmem((HALVES, plane, PER_HALF, ch, HEAD), F32),
            vmem((HALVES, plane, PER_HALF, ch, HEAD), F32),
            vmem((HALVES, nz, PER_HALF, ch, HEAD), BF16),
            vmem((HALVES, plane, PER_HALF, ch, HEAD), BF16),
            vmem((TOK, HQ * HEAD), BF16),
            vmem((TOK, wide), BF16),
            dma((2,)),
            dma((KEY_HEADS,)),
            dma((KEY_HEADS + 1,)),
            dma((KEY_HEADS,)),
            dma((KEY_HEADS,)),
            dma((2,)),
            dma((2,)),
            dma((2, KEY_HEADS)),
            dma((2, KEY_HEADS)),
            dma((12,)),
            dma((12,)),
        ],
        compiler_params=pltpu.CompilerParams(
            collective_id=0, has_side_effects=True, vmem_limit_bytes=40 * 2**20
        ),
    )(queries, packed_key_value, incoming, loss_grad, global_blocks, table)


def solution(mesh):
    n_sec, n_seq = mesh.shape["section"], mesh.shape["seq"]
    plane = math.isqrt(n_seq)
    in_specs = (
        P("section", "seq", None),
        P("section", "seq", None),
        P("section", "seq", None),
        P("seq", None),
        P("section", None),
        P("section", None, None, None),
    )
    out_specs = (P("section", "seq", None), P("section", "seq", None))
    return jax.shard_map(
        functools.partial(body, n_sec, plane, n_seq // plane),
        mesh=mesh, in_specs=in_specs, out_specs=out_specs, check_vma=False,
    )
```

time: 1480 us -> 98.4 us (0.07)
  blocking collectives: 981 us -> 0 us
  waiting for transfers between devices: 333 us -> 0 us
  Pallas kernels: 0 us -> 90.1 us
  matrix products: 84.4 us -> 0 us
  starting transfers between devices: 29.2 us -> 0 us
  local copies, waits for them, and re-layouts: 28.2 us -> 7.32 us
    psum x1 -> x0, blocking collectives: 981 us -> none  [body(): glob_rows = lax.psum(owned_rows, 'seq').astype(jnp.bfloat16)]
    psum x1 -> x0, waiting for transfers between devices: 333 us -> none  [body(): global_sum = lax.psum(glob_grads, 'seq')]
    pallas_call x0 -> x1, Pallas kernels: none -> 90.1 us  [body(): pl.pallas_call(functools.partial(kernel, n_sec, plane, nz), out_shape=(ja...]
    dot_general x22 -> x0, matrix products: 73.8 us -> none  [the longest x4 27.1 us: one_group(): jnp.einsum('xapt,xpag->xtg', score_gradient, query_grouped, preferred_ele...]
    ppermute x5 -> x0, starting transfers between devices: 29.1 us -> none  [the longest x2 23.8 us: with_halo(): after = lax.ppermute(first, axis, down)]
  transfers between devices with their start and end apart: 6 -> 0, of which waited for: 1 -> 0; matrix products, arithmetic and copies ran while one was open for 1% -> 0% of each run, Pallas kernels for 0% -> 0%
where the time goes in v1:
time: 98.4 us; the launch traced here: 98.1 us
  Pallas kernels  90.1 us (92%)
  local copies, waits for them, and re-layouts  7.32 us (7%)
    pallas_call x1, Pallas kernels, body(): pl.pallas_call(functools.partial(kernel, n_sec, plane, nz), out_shape=(ja...  90.1 us
    unnamed x14, local copies, waits for them, and re-layouts  7.32 us

profile of v1, /device:TPU:1, one launch (start us, length us, event | category | flops | bytes accessed | tf_op | source)
XLA Modules:
  0.0 98.1 jit_solution(18342100499143885892)
XLA Ops:
  0.6 0.0 copy-start.5
  0.6 0.6 copy-done.5
  1.3 0.0 copy-start
  1.3 1.1 %copy-done = bf16[1,128,3072]{2,1,0:T(8,128)(2,1)S(1)} copy-done((bf16[1,128,3072]{2,1,0:T(8,128)(2,1)S(1)}, bf16[1,128,3072]{2,1,0:T(8,128)(2,1)}, u32[]{:S(2)}) %copy-start) | copy-done | bytes 786456
  2.4 0.0 copy-start.1
  2.4 1.1 %copy-done.1 = bf16[1,128,3072]{2,1,0:T(8,128)(2,1)S(1)} copy-done((bf16[1,128,3072]{2,1,0:T(8,128)(2,1)S(1)}, bf16[1,128,3072]{2,1,0:T(8,128)(2,1)}, u32[]{:S(2)}) %copy-start.1) | copy-done | bytes 786456
  3.6 0.0 copy-start.2
  3.6 1.1 %copy-done.2 = bf16[128,3072]{1,0:T(8,128)(2,1)S(1)} copy-done((bf16[128,3072]{1,0:T(8,128)(2,1)S(1)}, bf16[128,3072]{1,0:T(8,128)(2,1)}, u32[]{:S(2)}) %copy-start.2) | copy-done | bytes 786456
  4.7 0.0 copy-start.3
  4.7 0.9 copy-done.3
  5.6 0.0 copy-start.4
  5.6 0.7 copy-done.4
  6.4 90.1 %shard_map.77 = (bf16[1,128,3072]{2,1,0:T(8,128)(2,1)S(1)}, bf16[1,128,1024]{2,1,0:T(8,128)(2,1)S(1)}) custom-call(bf16[1,128,3072]{2,1,0:T(8,128)(2,1)S(1)} %copy-done, bf16[1,128,1024]{2,1,0:T(8,128)(2,1)S(1)} %copy-done.3, bf16[1,128,3072]{2,1,0:T(8,128)(2,1)S(1)} %copy-done.1, bf16[128,3072]{1,0:T(8,128)(2,1)S(1)} %copy-done.2, s32[1,2]{1,0:T(1,128)S(1)} %copy-done.5, ...), custom_call_target="tpu_custom_call" | custom-call | tf_op jit(solution)/shard_map/pallas_call | solution.py:337
  96.5 0.9 copy.10
  97.4 0.7 copy.11
Async XLA Ops:
  0.6 0.7 copy-start.5
  1.3 1.1 %copy-start = (bf16[1,128,3072]{2,1,0:T(8,128)(2,1)S(1)}, bf16[1,128,3072]{2,1,0:T(8,128)(2,1)}, u32[]{:S(2)}) copy-start(bf16[1,128,3072]{2,1,0:T(8,128)(2,1)} %q_hbm.1) | copy-start | bytes 2359300
  2.4 1.1 %copy-start.1 = (bf16[1,128,3072]{2,1,0:T(8,128)(2,1)S(1)}, bf16[1,128,3072]{2,1,0:T(8,128)(2,1)}, u32[]{:S(2)}) copy-start(bf16[1,128,3072]{2,1,0:T(8,128)(2,1)} %inc_hbm.1) | copy-start | bytes 2359300
  3.6 1.1 %copy-start.2 = (bf16[128,3072]{1,0:T(8,128)(2,1)S(1)}, bf16[128,3072]{1,0:T(8,128)(2,1)}, u32[]{:S(2)}) copy-start(bf16[128,3072]{1,0:T(8,128)(2,1)} %loss_hbm.1) | copy-start | bytes 2359300
  4.7 0.9 copy-start.3
  5.6 0.7 copy-start.4

commit v2 on v1

--- a/solution.py
+++ b/solution.py
@@ -27,17 +27,17 @@
 
 def kernel(
     n_sec, plane, nz,
-    q_hbm, kv_hbm, inc_hbm, loss_hbm, gb_ref, rb_ref,
+    q_hbm, kv_hbm, inc_hbm, loss_hbm, gb_ref, rb_hbm,
     dq_hbm, dkv_hbm,
-    qv, dout, kvo, kvh, bias, kall, vall, kallt,
+    rb_ref, qv, dout, kvo, kvh, bias, kall, vall, kallt,
     g1src, r1a, r1b, r2a, r2b, gkv,
     acc, own, hgs, hgr, g2src, g2r1, g2r2, g2f, dqv, dkvv,
-    in_sem, loss_sem, out_sem,
+    in_sem, loss_sem, out_sem, kv_sem,
     sh_s, sh_r, ha_s, ha_r, hg_s, hg_r, pl_s, pl_r,
 ):
     n_seq = plane * nz
     r1, r2 = (r1a, r1b), (r2a, r2b)
-    ch = 4 * BLOCK // plane
+    ch = PER_HALF * 4 * BLOCK // plane
     rows = min(ch, BLOCK)
     s = lax.axis_index("section")
     q = lax.axis_index("seq")
@@ -48,29 +48,46 @@
     back = (lax.rem(s + n_sec - 1, n_sec), q)
     ahead = (lax.rem(s + 1, n_sec), q)
 
-    def plane_peer(i):
-        k = lax.rem(yc + i, plane)
-        return k, (s, z * plane + k)
-
-    def z_peer(i):
-        k = lax.rem(z + i, nz)
-        return k, (s, k * plane + yc)
-
-    barrier = pltpu.get_barrier_semaphore()
-    for peer in (right, left, back, ahead):
-        pl.semaphore_signal(barrier, inc=1, device_id=peer, device_id_type=MESH)
-
-    @pl.loop(1, plane)
-    def _(i):
-        pl.semaphore_signal(barrier, inc=1, device_id=plane_peer(i)[1], device_id_type=MESH)
-
-    @pl.loop(1, nz)
-    def _(i):
-        pl.semaphore_signal(barrier, inc=1, device_id=z_peer(i)[1], device_id_type=MESH)
+    def around(n, visit):
+        if n > 2:
+
+            @pl.loop(0, n // 2 - 1)
+            def _(t):
+                visit(n // 2 - t)
+                visit(n // 2 + 1 + t)
+
+        if n > 1:
+            visit(1)
+
+    def wrap(at, n):
+        return jnp.where(at >= n, at - n, at)
+
+    ny = plane // 4
+    y, c, zl = (q // 2) % ny, q % 2, yc // (2 * ny)
+
+    def plane_peers(act):
+        def at(off, skip=()):
+            row = wrap(y + off, ny) * 2
+            for dz, dc in ((1, 1), (1, 0), (0, 1), (0, 0)):
+                if (dz, dc) not in skip:
+                    k = (1 - zl if dz else zl) * (2 * ny) + row + (1 - c if dc else c)
+                    act(k, (s, z * plane + k))
+
+        around(ny, at)
+        at(0, ((0, 0),))
+
+    def z_peers(act):
+        def at(off):
+            k = wrap(z + off, nz)
+            act(k, (s, k * plane + yc))
+
+        around(nz, at)
 
     load_kv = pltpu.make_async_copy(kv_hbm.at[0], kvo, in_sem.at[0])
     load_q = pltpu.make_async_copy(q_hbm.at[0], qv, in_sem.at[1])
+    load_rb = pltpu.make_async_copy(rb_hbm, rb_ref, in_sem.at[2])
     load_kv.start()
+    load_rb.start()
     load_q.start()
 
     def cols(g):
@@ -84,17 +101,15 @@
         for g in range(KEY_HEADS):
             loss_copy(g).start()
 
-    pl.semaphore_wait(barrier, 4 + plane - 1 + nz - 1)
-
-    def shift(g):
-        return pltpu.make_async_remote_copy(
-            inc_hbm.at[0, :, cols(g)], dout.at[g], sh_s.at[g], sh_r.at[g], back, MESH
-        )
-
-    @pl.when(s > 0)
-    def _():
-        for g in range(KEY_HEADS):
-            shift(g).start()
+    barrier = pltpu.get_barrier_semaphore()
+    for peer in (right, left, back, ahead):
+        pl.semaphore_signal(barrier, inc=1, device_id=peer, device_id_type=MESH)
+
+    def greet(_, peer):
+        pl.semaphore_signal(barrier, inc=1, device_id=peer, device_id_type=MESH)
+
+    plane_peers(greet)
+    z_peers(greet)
 
     load_kv.wait()
     for j in range(2):
@@ -104,46 +119,57 @@
             for g in range(KEY_HEADS):
                 col = part * KEY_HEADS * HEAD + g * HEAD
                 for i in range(BLOCK // rows):
-                    at = part * 2 * BLOCK + j * BLOCK + i * rows
-                    g1src[g // PER_HALF, at // ch, g % PER_HALF, at % ch : at % ch + rows, :] = block[
+                    at = ((g % PER_HALF) * 4 + part * 2 + j) * BLOCK + i * rows
+                    g1src[g // PER_HALF, at // ch, at % ch : at % ch + rows, :] = block[
                         i * rows : (i + 1) * rows, col : col + HEAD
                     ]
 
+    pl.semaphore_wait(barrier, 4 + plane - 1 + nz - 1)
+
+    def shift(g):
+        return pltpu.make_async_remote_copy(
+            inc_hbm.at[0, :, cols(g)], dout.at[g], sh_s.at[g], sh_r.at[g], back, MESH
+        )
+
     def all_of(buf, count, sem):
         return pltpu.make_async_copy(buf.at[pl.ds(0, count)], buf.at[pl.ds(0, count)], sem)
 
     def plane_scatter(src, dst, row):
-        @pl.loop(1, plane)
-        def _(i):
-            k, peer = plane_peer(i)
+        def send(k, peer):
             pltpu.make_async_remote_copy(
                 src.at[k], dst.at[yc], pl_s.at[row], pl_r.at[row], peer, MESH
             ).start()
 
+        plane_peers(send)
+
     def plane_gather(buf, row):
-        @pl.loop(1, plane)
-        def _(i):
-            _, peer = plane_peer(i)
+        def send(_, peer):
             pltpu.make_async_remote_copy(
                 buf.at[yc], buf.at[yc], pl_s.at[row], pl_r.at[row], peer, MESH
             ).start()
 
+        plane_peers(send)
+
     def z_gather(buf, row):
-        @pl.loop(1, nz)
-        def _(i):
-            _, peer = z_peer(i)
+        def send(_, peer):
             pltpu.make_async_remote_copy(
                 buf.at[z], buf.at[z], pl_s.at[row], pl_r.at[row], peer, MESH
             ).start()
 
+        z_peers(send)
+
+    @pl.when(s > 0)
+    def _():
+        for g in range(KEY_HEADS):
+            shift(g).start()
+
     for h in range(HALVES):
         plane_scatter(g1src.at[h], r1[h], h)
 
     halo_right = pltpu.make_async_remote_copy(kv_hbm.at[0], kvh.at[0], ha_s.at[0], ha_r.at[0], right, MESH)
     halo_left = pltpu.make_async_remote_copy(kv_hbm.at[0], kvh.at[1], ha_s.at[1], ha_r.at[1], left, MESH)
-    halo_right.start()
-    halo_left.start()
-
+
+    load_rb.wait()
     table = rb_ref[...].astype(F32)
     lane = lax.broadcasted_iota(jnp.int32, table.shape, 2)
     first_block = (2 * (q - 1)).astype(F32)
@@ -178,14 +204,16 @@
         for sub in range(ch // rows):
             holder = lax.rem(owner(yc, sub), plane)
             part = r1[h][holder]
-            r2[h][z, :, sub * rows : (sub + 1) * rows, :] = part[:, sub * rows : (sub + 1) * rows, :]
+            r2[h][z, sub * rows : (sub + 1) * rows, :] = part[sub * rows : (sub + 1) * rows, :]
         z_gather(r2[h], 2 + h)
+    halo_right.start()
+    halo_left.start()
     for h in range(HALVES):
         all_of(r2[h], nz - 1, pl_r.at[2 + h]).wait()
         for sub in range(ch // rows):
             holder = owner(yc, sub) // plane
             part = r2[h][holder]
-            gkv[h, yc, :, sub * rows : (sub + 1) * rows, :] = part[:, sub * rows : (sub + 1) * rows, :]
+            gkv[h, yc, sub * rows : (sub + 1) * rows, :] = part[sub * rows : (sub + 1) * rows, :]
         plane_gather(gkv.at[h], 4 + h)
 
     load_q.wait()
@@ -201,6 +229,9 @@
             left if side == 0 else right, MESH,
         )
 
+    def quarter(gg, part):
+        return pl.ds((2 * gg + part) * (plane // 4), plane // 4)
+
     def one_group(h, gg):
         g = h * PER_HALF + gg
 
@@ -217,8 +248,7 @@
             dst[0:TOK, :] = kvh[0, :, col]
             dst[TOK : 2 * TOK, :] = kvo[:, col]
             dst[2 * TOK : 3 * TOK, :] = kvh[1, :, col]
-            half = plane // 2
-            dst[3 * TOK :, :] = gkv[h, part * half : (part + 1) * half, gg].reshape(2 * BLOCK, HEAD)
+            dst[3 * TOK :, :] = gkv[h, quarter(gg, part)].reshape(2 * BLOCK, HEAD)
         kallt[...] = kall[...].T
         acc[...] = jnp.zeros_like(acc)
         bias_row = bias[g]
@@ -257,11 +287,9 @@
         hgs[0, g] = acc[:, 0:TOK, :]
         own[g] = acc[:, TOK : 2 * TOK, :]
         hgs[1, g] = acc[:, 2 * TOK : 3 * TOK, :]
-        half = plane // 2
         for part in range(2):
-            g2src[h, part * half : (part + 1) * half, gg] = acc[part, 3 * TOK :, :].reshape(half, ch, HEAD)
-        halo_grad(0, g).start()
-        halo_grad(1, g).start()
+            sums = acc[part, 3 * TOK :, :].astype(BF16)
+            g2src[h, quarter(gg, part)] = sums.reshape(plane // 4, ch, HEAD)
 
     for h in range(HALVES):
         all_of(gkv.at[h], plane - 1, pl_r.at[4 + h]).wait()
@@ -271,22 +299,25 @@
             one_group(h, gg)
 
         plane_scatter(g2src.at[h], g2r1.at[h], 6 + h)
+        for g in range(h * PER_HALF, (h + 1) * PER_HALF):
+            halo_grad(0, g).start()
+            halo_grad(1, g).start()
 
     for h in range(HALVES):
         all_of(g2r1.at[h], plane - 1, pl_r.at[6 + h]).wait()
         g2r1[h, yc] = g2src[h, yc]
-        total = g2r1[h, 0]
-        for k in range(1, plane):
-            total += g2r1[h, k]
+        total = jnp.sum(g2r1[h].astype(F32), axis=0)
         g2r2[h, z] = total.astype(BF16)
         z_gather(g2r2.at[h], 8 + h)
     for h in range(HALVES):
         all_of(g2r2.at[h], nz - 1, pl_r.at[8 + h]).wait()
-        total = g2r2[h, 0].astype(F32)
-        for k in range(1, nz):
-            total += g2r2[h, k].astype(F32)
+        total = jnp.sum(g2r2[h].astype(F32), axis=0)
         g2f[h, yc] = total.astype(BF16)
         plane_gather(g2f.at[h], 10 + h)
+
+    def store_kv(h, part):
+        at = pl.ds((part * KEY_HEADS + h * PER_HALF) * HEAD, PER_HALF * HEAD)
+        return pltpu.make_async_copy(dkvv.at[:, at], dkv_hbm.at[0, :, at], kv_sem.at[h, part])
 
     for g in range(KEY_HEADS):
         for side in range(2):
@@ -295,11 +326,10 @@
         own[g] += hgr[0, g] + hgr[1, g]
     for h in range(HALVES):
         all_of(g2f.at[h], plane - 1, pl_r.at[10 + h]).wait()
-        half = plane // 2
         for gg in range(PER_HALF):
             g = h * PER_HALF + gg
             for part in range(2):
-                sums = g2f[h, part * half : (part + 1) * half, gg].reshape(2 * BLOCK, HEAD).astype(F32)
+                sums = g2f[h, quarter(gg, part)].reshape(2 * BLOCK, HEAD).astype(F32)
                 for n in range(2):
                     grad = own[g, part, n * BLOCK : (n + 1) * BLOCK, :]
                     for j in range(2):
@@ -307,8 +337,8 @@
                         grad += jnp.where(mine, sums[j * BLOCK : (j + 1) * BLOCK], 0.0)
                     col = (part * KEY_HEADS + g) * HEAD
                     dkvv[n * BLOCK : (n + 1) * BLOCK, col : col + HEAD] = grad.astype(BF16)
-    store_kv = pltpu.make_async_copy(dkvv, dkv_hbm.at[0], out_sem.at[KEY_HEADS])
-    store_kv.start()
+        for part in range(2):
+            store_kv(h, part).start()
 
     @pl.when(s > 0)
     def _():
@@ -324,11 +354,13 @@
         all_of(g2f.at[h], plane - 1, pl_s.at[10 + h]).wait()
     for g in range(KEY_HEADS):
         store_dq(g).wait()
-    store_kv.wait()
+    for h in range(HALVES):
+        for part in range(2):
+            store_kv(h, part).wait()
 
 
 def body(n_sec, plane, nz, queries, packed_key_value, incoming, loss_grad, global_blocks, random_blocks):
-    ch = 4 * BLOCK // plane
+    ch = PER_HALF * 4 * BLOCK // plane
     table = jnp.transpose(random_blocks[0], (2, 1, 0))
     anywhere = pl.BlockSpec(memory_space=pl.ANY)
     vmem = pltpu.VMEM
@@ -340,9 +372,10 @@
             jax.ShapeDtypeStruct(queries.shape, BF16),
             jax.ShapeDtypeStruct(packed_key_value.shape, BF16),
         ),
-        in_specs=[anywhere] * 4 + [pl.BlockSpec(memory_space=pltpu.SMEM), pl.BlockSpec(memory_space=pltpu.VMEM)],
+        in_specs=[anywhere] * 4 + [pl.BlockSpec(memory_space=pltpu.SMEM), anywhere],
         out_specs=(anywhere, anywhere),
         scratch_shapes=[
+            vmem(table.shape, jnp.int32),
             vmem((TOK, HQ * HEAD), BF16),
             vmem((KEY_HEADS, TOK, GROUP_COLS), BF16),
             vmem((TOK, wide), BF16),
@@ -351,25 +384,26 @@
             vmem((KEYS, HEAD), BF16),
             vmem((KEYS, HEAD), BF16),
             vmem((HEAD, KEYS), BF16),
-            vmem((HALVES, plane, PER_HALF, ch, HEAD), BF16),
-            vmem((plane, PER_HALF, ch, HEAD), BF16),
-            vmem((plane, PER_HALF, ch, HEAD), BF16),
-            vmem((nz, PER_HALF, ch, HEAD), BF16),
-            vmem((nz, PER_HALF, ch, HEAD), BF16),
-            vmem((HALVES, plane, PER_HALF, ch, HEAD), BF16),
+            vmem((HALVES, plane, ch, HEAD), BF16),
+            vmem((plane, ch, HEAD), BF16),
+            vmem((plane, ch, HEAD), BF16),
+            vmem((nz, ch, HEAD), BF16),
+            vmem((nz, ch, HEAD), BF16),
+            vmem((HALVES, plane, ch, HEAD), BF16),
             vmem((2, KEYS, HEAD), F32),
             vmem((KEY_HEADS, 2, TOK, HEAD), F32),
             vmem((2, KEY_HEADS, 2, TOK, HEAD), F32),
             vmem((2, KEY_HEADS, 2, TOK, HEAD), F32),
-            vmem((HALVES, plane, PER_HALF, ch, HEAD), F32),
-            vmem((HALVES, plane, PER_HALF, ch, HEAD), F32),
-            vmem((HALVES, nz, PER_HALF, ch, HEAD), BF16),
-            vmem((HALVES, plane, PER_HALF, ch, HEAD), BF16),
+            vmem((HALVES, plane, ch, HEAD), BF16),
+            vmem((HALVES, plane, ch, HEAD), BF16),
+            vmem((HALVES, nz, ch, HEAD), BF16),
+            vmem((HALVES, plane, ch, HEAD), BF16),
             vmem((TOK, HQ * HEAD), BF16),
             vmem((TOK, wide), BF16),
-            dma((2,)),
+            dma((3,)),
             dma((KEY_HEADS,)),
-            dma((KEY_HEADS + 1,)),
+            dma((KEY_HEADS,)),
+            dma((HALVES, 2)),
             dma((KEY_HEADS,)),
             dma((KEY_HEADS,)),
             dma((2,)),
@@ -380,14 +414,14 @@
             dma((12,)),
         ],
         compiler_params=pltpu.CompilerParams(
-            collective_id=0, has_side_effects=True, vmem_limit_bytes=40 * 2**20
+            collective_id=0, has_side_effects=True, vmem_limit_bytes=60 * 2**20
         ),
     )(queries, packed_key_value, incoming, loss_grad, global_blocks, table)
 
 
 def solution(mesh):
     n_sec, n_seq = mesh.shape["section"], mesh.shape["seq"]
-    plane = math.isqrt(n_seq)
+    plane = 2 * math.isqrt(n_seq)
     in_specs = (
         P("section", "seq", None),
         P("section", "seq", None),

time: 98.4 us -> 81 us (0.82)
  Pallas kernels: 90.1 us -> 77.4 us
  local copies, waits for them, and re-layouts: 7.32 us -> 2.81 us
    pallas_call x1, Pallas kernels: 90.1 us -> 77.4 us  [body(): pl.pallas_call(functools.partial(kernel, n_sec, plane, nz), out_shape=(ja...]
    unnamed x14 -> x4, local copies, waits for them, and re-layouts: 7.32 us -> 2.81 us
where the time goes in v2:
time: 81 us; the launch traced here: 80.8 us
  Pallas kernels  77.4 us (96%)
  local copies, waits for them, and re-layouts  2.81 us (3%)
    pallas_call x1, Pallas kernels, body(): pl.pallas_call(functools.partial(kernel, n_sec, plane, nz), out_shape=(ja...  77.4 us
    unnamed x4, local copies, waits for them, and re-layouts  2.81 us

profile of v2, /device:TPU:1, one launch (start us, length us, event | category | flops | bytes accessed | tf_op | source)
XLA Modules:
  0.0 80.8 jit_solution(918393119376680706)
XLA Ops:
  0.6 77.4 %shard_map.77 = (bf16[1,128,3072]{2,1,0:T(8,128)(2,1)}, bf16[1,128,1024]{2,1,0:T(8,128)(2,1)}) custom-call(bf16[1,128,3072]{2,1,0:T(8,128)(2,1)} %q_hbm.1, bf16[1,128,1024]{2,1,0:T(8,128)(2,1)} %kv_hbm.1, bf16[1,128,3072]{2,1,0:T(8,128)(2,1)} %inc_hbm.1, bf16[128,3072]{1,0:T(8,128)(2,1)} %loss_hbm.1, s32[1,2]{1,0:T(1,128)} %gb_ref.1, s32[3,4,512]{2,1,0:T(4,128)} %bitcast.3), custom_call_target="tpu_custom_call" | custom-call | tf_op jit(solution)/shard_map/pallas_call | solution.py:369
  78.0 0.0 copy-start
  78.0 2.1 %copy.10 = bf16[1,128,3072]{2,1,0:T(8,128)(2,1)} copy(bf16[1,128,3072]{2,1,0:T(8,128)(2,1)} %get-tuple-element.4) | data formatting | bytes 1572864
  80.1 0.0 copy-done
  80.1 0.7 copy.11
Async XLA Ops:
  78.0 2.1 %copy-start = (bf16[1,128,1024]{2,1,0:T(8,128)(2,1)S(1)}, bf16[1,128,1024]{2,1,0:T(8,128)(2,1)}, u32[]{:S(2)}) copy-start(bf16[1,128,1024]{2,1,0:T(8,128)(2,1)} %get-tuple-element.5) | copy-start | bytes 786436

commit v3 on v2

--- a/solution.py
+++ b/solution.py
@@ -102,14 +102,13 @@
             loss_copy(g).start()
 
     barrier = pltpu.get_barrier_semaphore()
-    for peer in (right, left, back, ahead):
-        pl.semaphore_signal(barrier, inc=1, device_id=peer, device_id_type=MESH)
-
     def greet(_, peer):
         pl.semaphore_signal(barrier, inc=1, device_id=peer, device_id_type=MESH)
 
+    z_peers(greet)
     plane_peers(greet)
-    z_peers(greet)
+    for peer in (right, left, back, ahead):
+        greet(0, peer)
 
     load_kv.wait()
     for j in range(2):
@@ -284,9 +283,9 @@
             dqv[:, pl.ds(pl.multiple_of(at + HEAD, HEAD), HEAD)] = dq_two[TOK:]
 
         store_dq(g).start()
-        hgs[0, g] = acc[:, 0:TOK, :]
+        hgs[0, g] = acc[:, 0:TOK, :].astype(BF16)
         own[g] = acc[:, TOK : 2 * TOK, :]
-        hgs[1, g] = acc[:, 2 * TOK : 3 * TOK, :]
+        hgs[1, g] = acc[:, 2 * TOK : 3 * TOK, :].astype(BF16)
         for part in range(2):
             sums = acc[part, 3 * TOK :, :].astype(BF16)
             g2src[h, quarter(gg, part)] = sums.reshape(plane // 4, ch, HEAD)
@@ -323,7 +322,7 @@
         for side in range(2):
             halo_grad(side, g).wait_send()
             halo_grad(side, g).wait_recv()
-        own[g] += hgr[0, g] + hgr[1, g]
+        own[g] += hgr[0, g].astype(F32) + hgr[1, g].astype(F32)
     for h in range(HALVES):
         all_of(g2f.at[h], plane - 1, pl_r.at[10 + h]).wait()
         for gg in range(PER_HALF):
@@ -392,8 +391,8 @@
             vmem((HALVES, plane, ch, HEAD), BF16),
             vmem((2, KEYS, HEAD), F32),
             vmem((KEY_HEADS, 2, TOK, HEAD), F32),
-            vmem((2, KEY_HEADS, 2, TOK, HEAD), F32),
-            vmem((2, KEY_HEADS, 2, TOK, HEAD), F32),
+            vmem((2, KEY_HEADS, 2, TOK, HEAD), BF16),
+            vmem((2, KEY_HEADS, 2, TOK, HEAD), BF16),
             vmem((HALVES, plane, ch, HEAD), BF16),
             vmem((HALVES, plane, ch, HEAD), BF16),
             vmem((HALVES, nz, ch, HEAD), BF16),

time: 81 us -> 79.7 us (0.984)
  Pallas kernels: 77.4 us -> 76 us
    pallas_call x1, Pallas kernels: 77.4 us -> 76 us  [body(): pl.pallas_call(functools.partial(kernel, n_sec, plane, nz), out_shape=(ja...]
where the time goes in v3:
time: 79.7 us; the launch traced here: 79.5 us
  Pallas kernels  76 us (95%)
  local copies, waits for them, and re-layouts  2.81 us (4%)
    pallas_call x1, Pallas kernels, body(): pl.pallas_call(functools.partial(kernel, n_sec, plane, nz), out_shape=(ja...  76 us
    unnamed x4, local copies, waits for them, and re-layouts  2.81 us

profile of v3, /device:TPU:1, one launch (start us, length us, event | category | flops | bytes accessed | tf_op | source)
XLA Modules:
  0.0 79.5 jit_solution(1848343778779639183)
XLA Ops:
  0.6 76.0 %shard_map.77 = (bf16[1,128,3072]{2,1,0:T(8,128)(2,1)}, bf16[1,128,1024]{2,1,0:T(8,128)(2,1)}) custom-call(bf16[1,128,3072]{2,1,0:T(8,128)(2,1)} %q_hbm.1, bf16[1,128,1024]{2,1,0:T(8,128)(2,1)} %kv_hbm.1, bf16[1,128,3072]{2,1,0:T(8,128)(2,1)} %inc_hbm.1, bf16[128,3072]{1,0:T(8,128)(2,1)} %loss_hbm.1, s32[1,2]{1,0:T(1,128)} %gb_ref.1, s32[3,4,512]{2,1,0:T(4,128)} %bitcast.3), custom_call_target="tpu_custom_call" | custom-call | tf_op jit(solution)/shard_map/pallas_call | solution.py:368
  76.7 0.0 copy-start
  76.7 2.1 %copy.10 = bf16[1,128,3072]{2,1,0:T(8,128)(2,1)} copy(bf16[1,128,3072]{2,1,0:T(8,128)(2,1)} %get-tuple-element.4) | data formatting | bytes 1572864
  78.8 0.0 copy-done
  78.8 0.7 copy.11
Async XLA Ops:
  76.7 2.1 %copy-start = (bf16[1,128,1024]{2,1,0:T(8,128)(2,1)S(1)}, bf16[1,128,1024]{2,1,0:T(8,128)(2,1)}, u32[]{:S(2)}) copy-start(bf16[1,128,1024]{2,1,0:T(8,128)(2,1)} %get-tuple-element.5) | copy-start | bytes 786436
